TPU v7x, 512 devices: a whole 4x8x8 slice. The times are simulated.
512 devices in a mesh: chan: 16 (over z, core), exp: 32 (over x, y).
Axes of the slice: x: 4, y: 8, z: 8, core: 2. Of those that a mesh axis runs over, the one named last changes fastest.
Arguments:
- tokens: bfloat16 [96, 256, 2048], P('chan', 'exp'), may hold values from -6 to 6
- kernel: float32 [3, 3, 2048], replicated, may hold values from -2 to 2
- gain: float32 [2048], replicated, may hold values from 0.1 to 1.9
- routes: int32 [24576, 2], P(('chan', 'exp')), may hold values from 0 to 63, all different within a row; in each aligned block of 48 rows (0 to 47, 48 to 95, ...) at most 2 rows name the same one
- gate_num: int32 [24576, 2], P(('chan', 'exp')), may hold values from 1 to 15
- gate_proj: bfloat16 [512, 176, 2048], P(('exp', 'chan')), may hold values from -0.125 to 0.125
- up_proj: bfloat16 [512, 176, 2048], P(('exp', 'chan')), may hold values from -0.125 to 0.125
- down_proj: bfloat16 [512, 176, 2048], P(('exp', 'chan')), may hold values from -0.15625 to 0.15625
Outputs:
- mixed: bfloat16 [96, 256, 2048], P('chan', 'exp')
Inputs may be any that keep to these rules, and one draw needn't show every extreme that they name: `routes`: the two ids of a row differ. Rows r * 48 to r * 48 + 47 are the tokens of one device, and in each such block no expert is named more than 2 times; some expert is named exactly 2 times in some blocks.
All inputs are finite; a program needn't handle non-finite values.
Results may differ from a plain program's by a relative error of at most 0.0085.
Values may be sent and summed in bfloat16 or wider, within the bound.
A program may use at most 64 MiB of HBM per device.

v0:
```python
import jax
import jax.numpy as jnp
from jax import lax
from jax.sharding import PartitionSpec as P

EXP_DEV = 2
eps = 1e-06


def with_halo(block, sides, width):
    for axis, dim in sides:
        count = lax.axis_size(axis)
        forward = [(i, i + 1) for i in range(count - 1)]
        backward = [(target, source) for source, target in forward]
        low = lax.ppermute(
            lax.slice_in_dim(block, block.shape[dim] - width, None, axis=dim), axis, forward
        )
        high = lax.ppermute(lax.slice_in_dim(block, 0, width, axis=dim), axis, backward)
        block = jnp.concatenate([low, block, high], axis=dim)
    return block


def depthwise(padded, kernel, row_count, col_count):
    image = padded.astype(jnp.float32)
    conv_sum = jnp.zeros((row_count, col_count, image.shape[2]), jnp.float32)
    for row_shift in range(3):
        for col_shift in range(3):
            conv_sum = (
                conv_sum
                + kernel[row_shift, col_shift]
                * image[row_shift : row_shift + row_count, col_shift : col_shift + col_count]
            )
    return conv_sum


def body(tokens, kernel, gain, routes, gate_num, gate_proj, up_proj, down_proj):
    row_count, col_count, width = tokens.shape
    padded = with_halo(tokens, (("chan", 0), ("exp", 1)), 1)
    conv_out = depthwise(padded, kernel, row_count, col_count)
    local_tokens = row_count * col_count
    flat_conv = conv_out.reshape(local_tokens, width)
    inverse_rms = lax.rsqrt(jnp.mean(flat_conv * flat_conv, axis=1, keepdims=True) + eps)
    normed = (flat_conv * inverse_rms * gain).astype(jnp.bfloat16)
    owners = lax.axis_size("exp")
    chan_count = lax.axis_size("chan")
    expert_count = EXP_DEV * owners
    capacity = 3 * local_tokens // expert_count
    slices = chan_count // EXP_DEV
    slot_count = expert_count * capacity
    route_pairs = routes.reshape(-1)
    onehot = (route_pairs[:, None] == jnp.arange(expert_count, dtype=jnp.int32)[None, :]).astype(
        jnp.int32
    )
    earlier = jnp.cumsum(onehot, axis=0) - onehot
    slot_rank = jnp.sum(earlier * onehot, axis=1)
    slot_index = (route_pairs % EXP_DEV * owners + route_pairs // EXP_DEV) * capacity + slot_rank
    chosen = (slot_index[:, None] == jnp.arange(slot_count, dtype=jnp.int32)[None, :]).reshape(
        local_tokens, 2, slot_count
    )
    placing = jnp.sum(chosen.astype(jnp.bfloat16), axis=1)
    outgoing = lax.dot_general(
        placing, normed, (((0,), (0,)), ((), ())), preferred_element_type=jnp.float32
    )
    outgoing = outgoing.astype(jnp.bfloat16).reshape(EXP_DEV, owners, capacity, width)
    arrived = lax.all_to_all(outgoing, "exp", split_axis=1, concat_axis=1, tiled=True)
    half_index = lax.axis_index("chan") // slices
    own_rows = lax.dynamic_index_in_dim(
        lax.all_gather(arrived, "chan", axis=1, tiled=True), half_index, 0, keepdims=False
    )
    block_shape = own_rows.shape
    flat_rows = own_rows.reshape(-1, width)
    gate_val = lax.dot_general(
        flat_rows, gate_proj[0], (((1,), (1,)), ((), ())), preferred_element_type=jnp.float32
    )
    up_val = lax.dot_general(
        flat_rows, up_proj[0], (((1,), (1,)), ((), ())), preferred_element_type=jnp.float32
    )
    hidden = (jax.nn.silu(gate_val) * up_val).astype(jnp.bfloat16)
    down_part = jnp.dot(hidden, down_proj[0], preferred_element_type=jnp.float32).astype(
        jnp.bfloat16
    )
    partial_rows = down_part.reshape(block_shape)
    partial_rows = partial_rows.reshape(chan_count, owners, capacity, width)
    returned = lax.all_to_all(partial_rows, "chan", split_axis=0, concat_axis=0, tiled=True)
    summed = jnp.sum(
        returned.reshape(EXP_DEV, slices, owners, capacity, width).astype(jnp.float32), axis=1
    ).astype(jnp.bfloat16)
    returned_rows = lax.all_to_all(summed, "exp", split_axis=1, concat_axis=1, tiled=True)
    numer = gate_num.astype(jnp.float32)
    fraction = numer / jnp.sum(numer, axis=1, keepdims=True)
    weighting = jnp.sum(chosen.astype(jnp.float32) * fraction[:, :, None], axis=1)
    moe_out = jnp.dot(
        weighting,
        returned_rows.reshape(slot_count, width).astype(jnp.float32),
        precision=lax.Precision.HIGHEST,
    )
    mixed = (flat_conv + moe_out).astype(jnp.bfloat16)
    return mixed.reshape(row_count, col_count, width)


def solution(mesh):
    return jax.shard_map(
        body,
        mesh=mesh,
        in_specs=(
            P("chan", "exp", None),
            P(),
            P(),
            P(("chan", "exp"), None),
            P(("chan", "exp"), None),
            P(("exp", "chan"), None, None),
            P(("exp", "chan"), None, None),
            P(("exp", "chan"), None, None),
        ),
        out_specs=P("chan", "exp", None),
        check_vma=False,
    )
```

profile of v0, /device:TPU:9, one launch (start us, length us, event | category | flops | bytes accessed | tf_op | source)
XLA Modules:
  0.0 289.5 jit_solution(8126721402879814620)
XLA Ops:
  6.5 0.0 copy-start
  6.5 0.0 copy-start.1
  6.5 0.0 all-gather.2.cloned.1.call-start
  6.5 0.9 fusion.41
  7.4 4.5 %collective-permute-start = (bf16[1,8,2048]{2,1,0:T(8,128)(2,1)S(1)}, bf16[1,8,2048]{2,1,0:T(8,128)(2,1)S(1)}, u32[]{:S(2)}, u32[]{:S(2)}) collective-permute-start(bf16[1,8,2048]{2,1,0:T(8,128)(2,1)S(1)} %get-tuple-element.10), channel_id=1, source_target_pairs={{0,32},{32,64},{64,96},{96,128},{128,160},{160,192},{192,224},{224... | collective-permute-start | bytes 98312 | tf_op jit(solution)/shard_map/ppermute | solution.py:15
  12.0 1.9 collective-permute-start.1
  13.9 0.8 copy.61
  14.7 0.7 broadcast_compare_fusion
  15.3 1.0 fusion.42
  16.4 0.1 eq.31
  16.5 0.1 fusion.28
  16.6 0.1 reduce_window_sum.11
  16.7 0.2 select_reduce_fusion.1
  16.9 0.1 reduce_sum.63
  17.0 0.1 copy.64
  17.2 0.1 copy.68
  17.3 0.0 collective-permute-done
  17.3 0.9 constant_dynamic-update-slice_fusion.1
  18.2 0.0 collective-permute-done.1
  18.2 0.1 fusion.40
  18.3 3.2 %collective-permute-start.2 = (bf16[8,1,2048]{2,1,0:T(2,128)(2,1)S(1)}, bf16[8,1,2048]{2,1,0:T(2,128)(2,1)S(1)}, u32[]{:S(2)}, u32[]{:S(2)}) collective-permute-start(bf16[8,1,2048]{2,1,0:T(2,128)(2,1)S(1)} %get-tuple-element.7), channel_id=1, source_target_pairs={{0,1},{1,2},{2,3},{3,4},{4,5},{5,6},{6,7},{7,8},{8,9},{9,10},{10,1... | collective-permute-start | bytes 98312 | tf_op jit(solution)/shard_map/ppermute | solution.py:15
  21.6 2.9 %collective-permute-start.3 = (bf16[8,1,2048]{2,1,0:T(2,128)(2,1)S(1)}, bf16[8,1,2048]{2,1,0:T(2,128)(2,1)S(1)}, u32[]{:S(2)}, u32[]{:S(2)}) collective-permute-start(bf16[8,1,2048]{2,1,0:T(2,128)(2,1)S(1)} %get-tuple-element.8), channel_id=1, source_target_pairs={{1,0},{2,1},{3,2},{4,3},{5,4},{6,5},{7,6},{8,7},{9,8},{10,9},{11,1... | collective-permute-start | bytes 98312 | tf_op jit(solution)/shard_map/ppermute | solution.py:18
  24.5 0.1 fusion.33
  24.6 0.2 collective-permute-done.2
  24.8 1.8 collective-permute-done.3
  26.6 0.2 maximum_convert_fusion
  26.8 0.6 multiply_reduce_fusion
  27.4 0.1 rsqrt.12
  27.5 0.0 copy-done.1
  27.5 0.4 convolution_convert_fusion.1
  27.9 0.3 reshape.99
  28.2 0.5 copy.69
  28.8 27.3 %all_to_all.15 = bf16[2,32,2,2048]{3,2,0,1:T(2,128)(2,1)} all-to-all(bf16[2,32,2,2048]{3,2,0,1:T(2,128)(2,1)S(1)} %copy.69), channel_id=1, replica_groups=mesh['chan'=16,'exp'=32] {'exp'}, dimensions={1} | all-to-all | bytes 1048576 | tf_op jit(solution)/shard_map/all_to_all | solution.py:65
  56.1 0.0 all-gather.2.cloned.1.call-update
  56.1 58.8 %all-gather.2.cloned.1.call-done = bf16[2,512,2,2048]{3,2,0,1:T(2,128)(2,1)} async-done(((bf16[2,32,2,2048]{3,2,0,1:T(2,128)(2,1)}), bf16[2,512,2,2048]{3,2,0,1:T(2,128)(2,1)}) %all-gather.2.cloned.1.call-update) | async-done | bytes 8388624 | tf_op jit(solution)/shard_map/all_gather | solution.py:68
  115.0 7.0 %constant_dynamic-slice_fusion = bf16[1,512,2,2048]{3,2,0,1:T(2,128)(2,1)} fusion(bf16[2,512,2,2048]{3,2,0,1:T(2,128)(2,1)} %all-gather.2.cloned.1.call-done, s32[]{:T(128)S(6)} %select_n.31), kind=kLoop, calls=%fused_computation.70 | loop fusion | bytes 8388612 | tf_op jit(solution)/shard_map/jit(dynamic_index_in_dim)/dynamic_slice | solution.py:67
  122.0 0.0 copy-start.3
  122.0 7.3 %reshape.100 = bf16[1024,2048]{1,0:T(8,128)(2,1)} reshape(bf16[1,512,2,2048]{3,2,0,1:T(2,128)(2,1)} %constant_dynamic-slice_fusion) | data formatting | bytes 8388608 | tf_op jit(solution)/shard_map/reshape | solution.py:71
  129.3 0.0 copy-done.3
  129.3 0.0 copy-start.4
  129.3 4.7 %fusion.6 = f32[1024,176]{0,1:T(8,128)} fusion(bf16[1024,2048]{1,0:T(8,128)(2,1)} %reshape.100, bf16[1,176,2048]{2,1,0:T(8,128)(2,1)S(1)} %copy-done.3), kind=kOutput, calls=%fused_computation.10 | convolution fusion | flops 738197504 | bytes 5636096 | tf_op jit(solution)/shard_map/dot_general | solution.py:72
  134.0 0.0 copy-done
  134.0 0.0 copy-done.4
  134.0 7.1 %convolution_convert_fusion = bf16[1024,2048]{1,0:T(8,128)(2,1)} fusion(bf16[1024,2048]{1,0:T(8,128)(2,1)} %reshape.100, bf16[1,176,2048]{2,1,0:T(8,128)(2,1)S(1)} %copy-done, bf16[1,176,2048]{2,1,0:T(8,128)(2,1)S(1)} %copy-done.4, f32[1024,176]{0,1:T(8,128)} %fusion.6), kind=kOutput, calls=%fused_computation.1 | convolution fusion | flops 1479573504 | bytes 10551296 | tf_op jit(solution)/shard_map/dot_general | solution.py:79
  141.1 7.6 %reshape_reshape.3 = bf16[16,32,2,2048]{3,2,1,0:T(2,128)(2,1)} reshape(bf16[1024,2048]{1,0:T(8,128)(2,1)} %convolution_convert_fusion) | data formatting | bytes 8388608 | tf_op jit(solution)/shard_map/reshape;reshape | solution.py:83
  148.7 100.3 %all_to_all.16 = bf16[16,32,2,2048]{3,2,1,0:T(2,128)(2,1)S(1)} all-to-all(bf16[16,32,2,2048]{3,2,1,0:T(2,128)(2,1)} %reshape_reshape.3), channel_id=1, replica_groups=mesh['chan'=16,'exp'=32] {'chan'}, dimensions={0} | all-to-all | bytes 8388608 | tf_op jit(solution)/shard_map/all_to_all | solution.py:84
  249.0 0.0 copy-start.2
  249.0 3.8 %bitcast_reduce_fusion = bf16[2,32,2,2048]{3,2,1,0:T(2,128)(2,1)S(1)} fusion(bf16[16,32,2,2048]{3,2,1,0:T(2,128)(2,1)S(1)} %all_to_all.16), kind=kLoop, calls=%fused_computation | loop fusion | flops 1835008 | bytes 4718592 | tf_op jit(solution)/shard_map/reduce_sum | solution.py:85
  252.9 1.4 copy.70
  254.2 9.3 %all-to-all-start.2 = ((bf16[2,32,2,2048]{3,2,0,1:T(2,128)(2,1)}), bf16[2,32,2,2048]{3,2,0,1:T(2,128)(2,1)S(1)}, u32[]{:S(2)}, u32[]{:S(2)}) async-start(bf16[2,32,2,2048]{3,2,0,1:T(2,128)(2,1)} %copy.70), calls=%async_computation.2 | async-start | bytes 1048576 | tf_op jit(solution)/shard_map/all_to_all | solution.py:88
  263.5 0.0 copy-done.2
  263.5 0.1 select_reduce_fusion
  263.6 17.4 %all-to-all-done.2 = bf16[2,32,2,2048]{3,2,0,1:T(2,128)(2,1)S(1)} async-done(((bf16[2,32,2,2048]{3,2,0,1:T(2,128)(2,1)}), bf16[2,32,2,2048]{3,2,0,1:T(2,128)(2,1)S(1)}, u32[]{:S(2)}, u32[]{:S(2)}) %all-to-all-start.2) | async-done | bytes 524320 | tf_op jit(solution)/shard_map/all_to_all | solution.py:88
  281.0 0.4 copy.71
  281.4 0.2 reshape.102
  281.6 1.0 fusion.1
  (6 shorter events, 0.1 us)
Async XLA Ops:
  6.5 127.5 %copy-start = (bf16[1,176,2048]{2,1,0:T(8,128)(2,1)S(1)}, bf16[1,176,2048]{2,1,0:T(8,128)(2,1)}, u32[]{:S(2)}) copy-start(bf16[1,176,2048]{2,1,0:T(8,128)(2,1)} %param.15) | copy-start | bytes 2162692
  6.5 21.0 %copy-start.1 = (f32[2048]{0:T(1024)S(1)}, f32[2048]{0:T(1024)}, u32[]{:S(2)}) copy-start(f32[2048]{0:T(1024)} %param.10) | copy-start | bytes 24580
  6.5 108.4 %all-gather.2.cloned.1.call-start = ((), (), s32[]{:S(2)}) async-start(), calls=%async_computation.3 | async-start | bytes 8912896 | tf_op jit(solution)/shard_map/all_gather | solution.py:68
  7.4 9.9 %collective-permute-start = (bf16[1,8,2048]{2,1,0:T(8,128)(2,1)S(1)}, bf16[1,8,2048]{2,1,0:T(8,128)(2,1)S(1)}, u32[]{:S(2)}, u32[]{:S(2)}) collective-permute-start(bf16[1,8,2048]{2,1,0:T(8,128)(2,1)S(1)} %get-tuple-element.10), channel_id=1, source_target_pairs={{0,32},{32,64},{64,96},{96,128},{128,160},{160,192},{192,224},{224... | collective-permute-start | bytes 98312 | tf_op jit(solution)/shard_map/ppermute | solution.py:15
  12.0 6.3 %collective-permute-start.1 = (bf16[1,8,2048]{2,1,0:T(8,128)(2,1)S(1)}, bf16[1,8,2048]{2,1,0:T(8,128)(2,1)S(1)}, u32[]{:S(2)}, u32[]{:S(2)}) collective-permute-start(bf16[1,8,2048]{2,1,0:T(8,128)(2,1)S(1)} %get-tuple-element.9), channel_id=1, source_target_pairs={{32,0},{64,32},{96,64},{128,96},{160,128},{192,160},{224,192},{256... | collective-permute-start | bytes 98312 | tf_op jit(solution)/shard_map/ppermute | solution.py:18
  18.3 6.4 %collective-permute-start.2 = (bf16[8,1,2048]{2,1,0:T(2,128)(2,1)S(1)}, bf16[8,1,2048]{2,1,0:T(2,128)(2,1)S(1)}, u32[]{:S(2)}, u32[]{:S(2)}) collective-permute-start(bf16[8,1,2048]{2,1,0:T(2,128)(2,1)S(1)} %get-tuple-element.7), channel_id=1, source_target_pairs={{0,1},{1,2},{2,3},{3,4},{4,5},{5,6},{6,7},{7,8},{8,9},{9,10},{10,1... | collective-permute-start | bytes 98312 | tf_op jit(solution)/shard_map/ppermute | solution.py:15
  21.6 5.0 %collective-permute-start.3 = (bf16[8,1,2048]{2,1,0:T(2,128)(2,1)S(1)}, bf16[8,1,2048]{2,1,0:T(2,128)(2,1)S(1)}, u32[]{:S(2)}, u32[]{:S(2)}) collective-permute-start(bf16[8,1,2048]{2,1,0:T(2,128)(2,1)S(1)} %get-tuple-element.8), channel_id=1, source_target_pairs={{1,0},{2,1},{3,2},{4,3},{5,4},{6,5},{7,6},{8,7},{9,8},{10,9},{11,1... | collective-permute-start | bytes 98312 | tf_op jit(solution)/shard_map/ppermute | solution.py:18
  122.0 7.3 %copy-start.3 = (bf16[1,176,2048]{2,1,0:T(8,128)(2,1)S(1)}, bf16[1,176,2048]{2,1,0:T(8,128)(2,1)}, u32[]{:S(2)}) copy-start(bf16[1,176,2048]{2,1,0:T(8,128)(2,1)} %param.13) | copy-start | bytes 2162692
  129.3 4.7 %copy-start.4 = (bf16[1,176,2048]{2,1,0:T(8,128)(2,1)S(1)}, bf16[1,176,2048]{2,1,0:T(8,128)(2,1)}, u32[]{:S(2)}) copy-start(bf16[1,176,2048]{2,1,0:T(8,128)(2,1)} %param.14) | copy-start | bytes 2162692
  249.0 14.5 %copy-start.2 = (s32[48,2]{0,1:T(2,128)S(1)}, s32[48,2]{0,1:T(2,128)}, u32[]{:S(2)}) copy-start(s32[48,2]{0,1:T(2,128)} %param.12) | copy-start | bytes 1156
  254.2 26.8 %all-to-all-start.2 = ((bf16[2,32,2,2048]{3,2,0,1:T(2,128)(2,1)}), bf16[2,32,2,2048]{3,2,0,1:T(2,128)(2,1)S(1)}, u32[]{:S(2)}, u32[]{:S(2)}) async-start(bf16[2,32,2,2048]{3,2,0,1:T(2,128)(2,1)} %copy.70), calls=%async_computation.2 | async-start | bytes 1048576 | tf_op jit(solution)/shard_map/all_to_all | solution.py:88
Sparse Core Ops, SparseCore 0:
  56.2 58.6 all-gather.1
where the time goes:
time: 290 us; the launch traced here: 289 us
  blocking collectives  128 us (44%)
  waiting for transfers between devices  78.2 us (27%)
  local copies, waits for them, and re-layouts  29 us (10%)
  starting transfers between devices  21.9 us (8%)
  between operations  13.6 us (5%)
  matrix products  13.2 us (5%)
  other arithmetic  5.98 us (2%)
    all_to_all x1, blocking collectives, body(): lax.all_to_all(partial_rows, 'chan', split_axis=0, concat_axis=0, tiled=T...  100 us
    all_gather x1, waiting for transfers between devices, body(): lax.all_gather(arrived, 'chan', axis=1, tiled=True)  58.8 us
    all_to_all x1, blocking collectives, body(): lax.all_to_all(outgoing, 'exp', split_axis=1, concat_axis=1, tiled=True)  27.3 us
    all_to_all x1, waiting for transfers between devices, body(): lax.all_to_all(summed, 'exp', split_axis=1, concat_axis=1, tiled=True)  17.4 us
    all_to_all x1, starting transfers between devices, body(): lax.all_to_all(summed, 'exp', split_axis=1, concat_axis=1, tiled=True)  9.28 us
    ppermute x2, starting transfers between devices, with_halo(): lax.ppermute(lax.slice_in_dim(block, block.shape[dim] - width, None, axis...  7.75 us
    another operation x1, local copies, waits for them, and re-layouts, body(): partial_rows = partial_rows.reshape(chan_count, owners, capacity, width)  7.62 us
    reshape x1, local copies, waits for them, and re-layouts, body(): flat_rows = own_rows.reshape(-1, width)  7.28 us
  transfers between devices with their start and end apart: 6, of which 4 were waited for; matrix products, arithmetic and copies ran while one was open for 2% of the time, Pallas kernels for 0%

commit v1 on v0

--- a/solution.py
+++ b/solution.py
@@ -1,10 +1,34 @@
+import functools
 import jax
 import jax.numpy as jnp
 from jax import lax
 from jax.sharding import PartitionSpec as P
+from jax.lax import axis_index, axis_size, ppermute
 
 EXP_DEV = 2
 eps = 1e-06
+
+
+def enter_files_on_mesh(matrix, axis_no):
+    n_dev_all = axis_size("chan")
+    x_next = map(lambda q: (q, (q + 1) % n_dev_all), range(n_dev_all))
+    fields = list(x_next)
+    block_now = map(lambda q: (q, (q - 1) % n_dev_all), range(n_dev_all))
+    buffer = list(block_now)
+    tile_out, row_out = ([matrix], [matrix])
+    for _ in range(n_dev_all // 2):
+        piece_out = ppermute(tile_out[-1], "chan", fields)
+        tile_out.append(piece_out)
+    ix = 0
+    while ix < (n_dev_all - 1) // 2:
+        row_out.append(ppermute(row_out[-1], "chan", buffer))
+        ix += 1
+    y2 = jnp.concatenate([*tile_out[::-1], *row_out[1:]], axis_no)
+    b_now = jnp.roll(y2, (axis_index("chan") - n_dev_all // 2) * matrix.shape[axis_no], axis_no)
+    return b_now
+
+
+feed_units_in = functools.partial(enter_files_on_mesh, axis_no=1)
 
 
 def with_halo(block, sides, width):
@@ -64,9 +88,7 @@
     outgoing = outgoing.astype(jnp.bfloat16).reshape(EXP_DEV, owners, capacity, width)
     arrived = lax.all_to_all(outgoing, "exp", split_axis=1, concat_axis=1, tiled=True)
     half_index = lax.axis_index("chan") // slices
-    own_rows = lax.dynamic_index_in_dim(
-        lax.all_gather(arrived, "chan", axis=1, tiled=True), half_index, 0, keepdims=False
-    )
+    own_rows = lax.dynamic_index_in_dim(feed_units_in(arrived), half_index, 0, keepdims=False)
     block_shape = own_rows.shape
     flat_rows = own_rows.reshape(-1, width)
     gate_val = lax.dot_general(

time: 290 us -> 356 us (1.23)
  local copies, waits for them, and re-layouts: 29 us -> 87 us
  starting transfers between devices: 21.9 us -> 49.3 us
  waiting for transfers between devices: 78.2 us -> 57 us
  blocking collectives: 128 us -> 142 us
  between operations: 13.6 us -> 0.28 us
    all_gather x1 -> x0, waiting for transfers between devices: 58.8 us -> none  [body(): lax.all_gather(arrived, 'chan', axis=1, tiled=True)]
    unnamed x13 -> x70, local copies, waits for them, and re-layouts: 1.74 us -> 58.6 us
    ppermute x0 -> x15, waiting for transfers between devices: none -> 37.6 us  [the longest x8 32.5 us: enter_files_on_mesh(): piece_out = ppermute(tile_out[-1], 'chan', fields)]
    ppermute x0 -> x15, starting transfers between devices: none -> 32.4 us  [the longest x8 21.3 us: enter_files_on_mesh(): piece_out = ppermute(tile_out[-1], 'chan', fields)]
    all_to_all x1, blocking collectives: 100 us -> 114 us  [body(): lax.all_to_all(partial_rows, 'chan', split_axis=0, concat_axis=0, tiled=T...]
    all_to_all x1, starting transfers between devices: 9.28 us -> 4.29 us  [body(): lax.all_to_all(summed, 'exp', split_axis=1, concat_axis=1, tiled=True)]
  transfers between devices with their start and end apart: 6 -> 20, of which waited for: 4 -> 16; matrix products, arithmetic and copies ran while one was open for 2% -> 10% of each run, Pallas kernels for 0% -> 0%
where the time goes in v1:
time: 356 us; the launch traced here: 354 us
  blocking collectives  142 us (40%)
  local copies, waits for them, and re-layouts  87 us (24%)
  waiting for transfers between devices  57 us (16%)
  starting transfers between devices  49.3 us (14%)
  matrix products  13.2 us (4%)
  other arithmetic  5.98 us (2%)
    all_to_all x1, blocking collectives, body(): lax.all_to_all(partial_rows, 'chan', split_axis=0, concat_axis=0, tiled=T...  114 us
    unnamed x70, local copies, waits for them, and re-layouts  58.6 us
    ppermute x8, waiting for transfers between devices, enter_files_on_mesh(): piece_out = ppermute(tile_out[-1], 'chan', fields)  32.5 us
    all_to_all x1, blocking collectives, body(): lax.all_to_all(outgoing, 'exp', split_axis=1, concat_axis=1, tiled=True)  27.2 us
    ppermute x8, starting transfers between devices, enter_files_on_mesh(): piece_out = ppermute(tile_out[-1], 'chan', fields)  21.3 us
    all_to_all x1, waiting for transfers between devices, body(): lax.all_to_all(summed, 'exp', split_axis=1, concat_axis=1, tiled=True)  17.4 us
    ppermute x7, starting transfers between devices, enter_files_on_mesh(): row_out.append(ppermute(row_out[-1], 'chan', buffer))  11.1 us
    ppermute x2, starting transfers between devices, with_halo(): lax.ppermute(lax.slice_in_dim(block, block.shape[dim] - width, None, axis...  7.75 us
  transfers between devices with their start and end apart: 20, of which 16 were waited for; matrix products, arithmetic and copies ran while one was open for 10% of the time, Pallas kernels for 0%

profile of v1, /device:TPU:9, one launch (start us, length us, event | category | flops | bytes accessed | tf_op | source)
XLA Modules:
  0.0 354.2 jit_solution(7514901632915786380)
XLA Ops:
  0.9 4.5 %collective-permute-start = (bf16[1,8,2048]{2,1,0:T(8,128)(2,1)S(1)}, bf16[1,8,2048]{2,1,0:T(8,128)(2,1)S(1)}, u32[]{:S(2)}, u32[]{:S(2)}) collective-permute-start(bf16[1,8,2048]{2,1,0:T(8,128)(2,1)S(1)} %get-tuple-element.10), channel_id=1, source_target_pairs={{0,32},{32,64},{64,96},{96,128},{128,160},{160,192},{192,224},{224... | collective-permute-start | bytes 98312 | tf_op jit(solution)/shard_map/ppermute | solution.py:39
  5.4 1.9 collective-permute-start.1
  11.8 3.2 collective-permute-start.2
  15.0 2.9 collective-permute-start.3
  18.2 1.8 collective-permute-done.3
  22.9 27.2 %all_to_all.15 = bf16[2,32,2,2048]{3,2,0,1:T(2,128)(2,1)S(1)} all-to-all(bf16[2,32,2,2048]{3,2,0,1:T(2,128)(2,1)S(1)} %copy.69), channel_id=1, replica_groups=mesh['chan'=16,'exp'=32] {'exp'}, dimensions={1} | all-to-all | bytes 1048576 | tf_op jit(solution)/shard_map/all_to_all | solution.py:89
  50.1 3.8 %collective-permute-start.4 = (bf16[2,32,2,2048]{3,2,0,1:T(2,128)(2,1)S(1)}, bf16[2,32,2,2048]{3,2,0,1:T(2,128)(2,1)S(1)}, u32[]{:S(2)}, u32[]{:S(2)}) collective-permute-start(bf16[2,32,2,2048]{3,2,0,1:T(2,128)(2,1)S(1)} %all_to_all.15), channel_id=1, source_target_pairs={{0,32},{32,64},{64,96},{96,128},{128,160},{160,192},{192,224},{224... | collective-permute-start | bytes 1572872 | tf_op jit(solution)/shard_map/ppermute | solution.py:20
  53.9 6.1 %collective-permute-done.4 = bf16[2,32,2,2048]{3,2,0,1:T(2,128)(2,1)S(1)} collective-permute-done((bf16[2,32,2,2048]{3,2,0,1:T(2,128)(2,1)S(1)}, bf16[2,32,2,2048]{3,2,0,1:T(2,128)(2,1)S(1)}, u32[]{:S(2)}, u32[]{:S(2)}) %collective-permute-start.4) | collective-permute-done | bytes 524320 | tf_op jit(solution)/shard_map/ppermute | solution.py:20
  60.1 2.5 collective-permute-start.5
  62.6 6.1 %collective-permute-done.5 = bf16[2,32,2,2048]{3,2,0,1:T(2,128)(2,1)S(1)} collective-permute-done((bf16[2,32,2,2048]{3,2,0,1:T(2,128)(2,1)S(1)}, bf16[2,32,2,2048]{3,2,0,1:T(2,128)(2,1)S(1)}, u32[]{:S(2)}, u32[]{:S(2)}) %collective-permute-start.5) | collective-permute-done | bytes 524320 | tf_op jit(solution)/shard_map/ppermute | solution.py:20
  68.7 2.5 collective-permute-start.6
  71.2 6.1 %collective-permute-done.6 = bf16[2,32,2,2048]{3,2,0,1:T(2,128)(2,1)S(1)} collective-permute-done((bf16[2,32,2,2048]{3,2,0,1:T(2,128)(2,1)S(1)}, bf16[2,32,2,2048]{3,2,0,1:T(2,128)(2,1)S(1)}, u32[]{:S(2)}, u32[]{:S(2)}) %collective-permute-start.6) | collective-permute-done | bytes 524320 | tf_op jit(solution)/shard_map/ppermute | solution.py:20
  77.3 2.5 collective-permute-start.7
  80.7 5.2 %collective-permute-done.7 = bf16[2,32,2,2048]{3,2,0,1:T(2,128)(2,1)S(1)} collective-permute-done((bf16[2,32,2,2048]{3,2,0,1:T(2,128)(2,1)S(1)}, bf16[2,32,2,2048]{3,2,0,1:T(2,128)(2,1)S(1)}, u32[]{:S(2)}, u32[]{:S(2)}) %collective-permute-start.7) | collective-permute-done | bytes 524320 | tf_op jit(solution)/shard_map/ppermute | solution.py:20
  85.9 2.5 collective-permute-start.8
  88.8 1.3 collective-permute-start.15
  90.1 4.4 %collective-permute-done.8 = bf16[2,32,2,2048]{3,2,0,1:T(2,128)(2,1)S(1)} collective-permute-done((bf16[2,32,2,2048]{3,2,0,1:T(2,128)(2,1)S(1)}, bf16[2,32,2,2048]{3,2,0,1:T(2,128)(2,1)S(1)}, u32[]{:S(2)}, u32[]{:S(2)}) %collective-permute-start.8) | collective-permute-done | bytes 524320 | tf_op jit(solution)/shard_map/ppermute | solution.py:20
  94.5 2.5 collective-permute-start.9
  98.5 2.3 collective-permute-start.16
  100.8 2.4 collective-permute-done.9
  103.1 2.5 collective-permute-start.10
  105.6 1.8 collective-permute-done.16
  107.4 3.0 collective-permute-start.17
  110.4 1.4 collective-permute-done.10
  111.7 2.6 collective-permute-start.11
  114.4 2.2 collective-permute-done.17
  116.6 4.0 %collective-permute-start.18 = (bf16[2,32,2,2048]{3,2,0,1:T(2,128)(2,1)}, bf16[2,32,2,2048]{3,2,0,1:T(2,128)(2,1)S(1)}, u32[]{:S(2)}, u32[]{:S(2)}) collective-permute-start(bf16[2,32,2,2048]{3,2,0,1:T(2,128)(2,1)} %collective-permute-done.17), channel_id=1, source_target_pairs={{0,480},{32,0},{64,32},{96,64},{128,96},{160,128},{192,160},{224,1... | collective-permute-start | bytes 1572872 | tf_op jit(solution)/shard_map/ppermute | solution.py:24
  121.4 2.3 constant_dynamic-update-slice_fusion.34
  123.7 2.3 constant_dynamic-update-slice_fusion.33
  126.0 2.3 constant_dynamic-update-slice_fusion.32
  128.2 2.3 constant_dynamic-update-slice_fusion.31
  130.5 2.3 constant_dynamic-update-slice_fusion.30
  132.8 2.3 constant_dynamic-update-slice_fusion.29
  135.1 2.3 constant_dynamic-update-slice_fusion.28
  138.6 1.3 constant_dynamic-update-slice_fusion.26
  141.1 2.3 constant_dynamic-update-slice_fusion.24
  143.4 2.3 constant_dynamic-update-slice_fusion.23
  145.7 2.3 constant_dynamic-update-slice_fusion.22
  147.9 2.3 constant_dynamic-update-slice_fusion.21
  150.2 2.3 constant_dynamic-update-slice_fusion.20
  152.5 1.3 constant_dynamic-update-slice_fusion.19
  153.8 2.3 constant_dynamic-update-slice_fusion.18
  156.1 2.3 constant_dynamic-update-slice_fusion.17
  158.4 1.3 constant_dynamic-update-slice_fusion.16
  159.7 1.3 constant_dynamic-update-slice_fusion.15
  161.0 1.3 constant_dynamic-update-slice_fusion.14
  162.2 1.3 constant_dynamic-update-slice_fusion.13
  163.5 1.3 constant_dynamic-update-slice_fusion.12
  164.7 1.3 constant_dynamic-update-slice_fusion.11
  166.0 1.3 constant_dynamic-update-slice_fusion.10
  168.5 1.3 constant_dynamic-update-slice_fusion.8
  169.8 1.3 constant_dynamic-update-slice_fusion.7
  172.3 2.5 constant_dynamic-update-slice_fusion.5
  174.8 2.3 constant_dynamic-update-slice_fusion.4
  178.3 7.0 %constant_dynamic-slice_fusion = bf16[1,512,2,2048]{3,2,0,1:T(2,128)(2,1)} fusion(bf16[2,1024,2,2048]{3,2,0,1:T(2,128)(2,1)} %constant_dynamic-update-slice_fusion.3, s32[]{:T(128)S(6)} %select_n.48, s32[]{:T(128)S(6)} %select_n.51), kind=kLoop, calls=%fused_computation.97 | loop fusion | bytes 8388616 | tf_op jit(solution)/shard_map/jit(dynamic_index_in_dim)/dynamic_slice | solution.py:91
  185.3 7.2 %reshape.100 = bf16[1024,2048]{1,0:T(8,128)(2,1)} reshape(bf16[1,512,2,2048]{3,2,0,1:T(2,128)(2,1)} %constant_dynamic-slice_fusion) | data formatting | bytes 8388608 | tf_op jit(solution)/shard_map/reshape | solution.py:93
  192.5 3.9 %fusion.3 = f32[1024,176]{0,1:T(8,128)S(1)} fusion(bf16[1024,2048]{1,0:T(8,128)(2,1)} %reshape.100, bf16[1,176,2048]{2,1,0:T(8,128)(2,1)} %param.14), kind=kOutput, calls=%fused_computation.7 | convolution fusion | flops 738197504 | bytes 5636096 | tf_op jit(solution)/shard_map/dot_general | solution.py:97
  196.4 7.2 %convolution_convert_fusion = bf16[1024,2048]{1,0:T(8,128)(2,1)} fusion(bf16[1,176,2048]{2,1,0:T(8,128)(2,1)S(1)} %copy-done, f32[1024,176]{0,1:T(8,128)S(1)} %fusion.3, bf16[1024,2048]{1,0:T(8,128)(2,1)} %reshape.100, bf16[1,176,2048]{2,1,0:T(8,128)(2,1)} %param.13), kind=kOutput, calls=%fused_computation.1 | convolution fusion | flops 1479573504 | bytes 10551296 | tf_op jit(solution)/shard_map/dot_general | solution.py:101
  203.6 7.6 %reshape_reshape.3 = bf16[16,32,2,2048]{3,2,1,0:T(2,128)(2,1)} reshape(bf16[1024,2048]{1,0:T(8,128)(2,1)} %convolution_convert_fusion) | data formatting | bytes 8388608 | tf_op jit(solution)/shard_map/reshape;reshape | solution.py:105
  211.2 114.4 %all_to_all.16 = bf16[16,32,2,2048]{3,2,1,0:T(2,128)(2,1)S(1)} all-to-all(bf16[16,32,2,2048]{3,2,1,0:T(2,128)(2,1)} %reshape_reshape.3), channel_id=1, replica_groups=mesh['chan'=16,'exp'=32] {'chan'}, dimensions={0} | all-to-all | bytes 8388608 | tf_op jit(solution)/shard_map/all_to_all | solution.py:106
  325.6 3.8 %bitcast_reduce_fusion = bf16[2,32,2,2048]{3,2,1,0:T(2,128)(2,1)S(1)} fusion(bf16[16,32,2,2048]{3,2,1,0:T(2,128)(2,1)S(1)} %all_to_all.16), kind=kLoop, calls=%fused_computation | loop fusion | flops 1835008 | bytes 4718592 | tf_op jit(solution)/shard_map/reduce_sum | solution.py:107
  329.4 1.4 copy.70
  330.8 4.3 %all-to-all-start.2 = ((bf16[2,32,2,2048]{3,2,0,1:T(2,128)(2,1)}), bf16[2,32,2,2048]{3,2,0,1:T(2,128)(2,1)S(1)}, u32[]{:S(2)}, u32[]{:S(2)}) async-start(bf16[2,32,2,2048]{3,2,0,1:T(2,128)(2,1)} %copy.70), calls=%async_computation.2 | async-start | bytes 1048576 | tf_op jit(solution)/shard_map/all_to_all | solution.py:110
  335.2 17.4 %all-to-all-done.2 = bf16[2,32,2,2048]{3,2,0,1:T(2,128)(2,1)S(1)} async-done(((bf16[2,32,2,2048]{3,2,0,1:T(2,128)(2,1)}), bf16[2,32,2,2048]{3,2,0,1:T(2,128)(2,1)S(1)}, u32[]{:S(2)}, u32[]{:S(2)}) %all-to-all-start.2) | async-done | bytes 524320 | tf_op jit(solution)/shard_map/all_to_all | solution.py:110
  (83 shorter events, 19.9 us)
Async XLA Ops:
  0.0 196.4 %copy-start = (bf16[1,176,2048]{2,1,0:T(8,128)(2,1)S(1)}, bf16[1,176,2048]{2,1,0:T(8,128)(2,1)}, u32[]{:S(2)}) copy-start(bf16[1,176,2048]{2,1,0:T(8,128)(2,1)} %param.15) | copy-start | bytes 2162692
  0.9 9.9 %collective-permute-start = (bf16[1,8,2048]{2,1,0:T(8,128)(2,1)S(1)}, bf16[1,8,2048]{2,1,0:T(8,128)(2,1)S(1)}, u32[]{:S(2)}, u32[]{:S(2)}) collective-permute-start(bf16[1,8,2048]{2,1,0:T(8,128)(2,1)S(1)} %get-tuple-element.10), channel_id=1, source_target_pairs={{0,32},{32,64},{64,96},{96,128},{128,160},{160,192},{192,224},{224... | collective-permute-start | bytes 98312 | tf_op jit(solution)/shard_map/ppermute | solution.py:39
  5.4 6.3 %collective-permute-start.1 = (bf16[1,8,2048]{2,1,0:T(8,128)(2,1)S(1)}, bf16[1,8,2048]{2,1,0:T(8,128)(2,1)S(1)}, u32[]{:S(2)}, u32[]{:S(2)}) collective-permute-start(bf16[1,8,2048]{2,1,0:T(8,128)(2,1)S(1)} %get-tuple-element.9), channel_id=1, source_target_pairs={{32,0},{64,32},{96,64},{128,96},{160,128},{192,160},{224,192},{256... | collective-permute-start | bytes 98312 | tf_op jit(solution)/shard_map/ppermute | solution.py:42
  11.8 6.4 %collective-permute-start.2 = (bf16[8,1,2048]{2,1,0:T(2,128)(2,1)S(1)}, bf16[8,1,2048]{2,1,0:T(2,128)(2,1)S(1)}, u32[]{:S(2)}, u32[]{:S(2)}) collective-permute-start(bf16[8,1,2048]{2,1,0:T(2,128)(2,1)S(1)} %get-tuple-element.7), channel_id=1, source_target_pairs={{0,1},{1,2},{2,3},{3,4},{4,5},{5,6},{6,7},{7,8},{8,9},{9,10},{10,1... | collective-permute-start | bytes 98312 | tf_op jit(solution)/shard_map/ppermute | solution.py:39
  15.0 5.0 %collective-permute-start.3 = (bf16[8,1,2048]{2,1,0:T(2,128)(2,1)S(1)}, bf16[8,1,2048]{2,1,0:T(2,128)(2,1)S(1)}, u32[]{:S(2)}, u32[]{:S(2)}) collective-permute-start(bf16[8,1,2048]{2,1,0:T(2,128)(2,1)S(1)} %get-tuple-element.8), channel_id=1, source_target_pairs={{1,0},{2,1},{3,2},{4,3},{5,4},{6,5},{7,6},{8,7},{9,8},{10,9},{11,1... | collective-permute-start | bytes 98312 | tf_op jit(solution)/shard_map/ppermute | solution.py:42
  50.1 9.9 %collective-permute-start.4 = (bf16[2,32,2,2048]{3,2,0,1:T(2,128)(2,1)S(1)}, bf16[2,32,2,2048]{3,2,0,1:T(2,128)(2,1)S(1)}, u32[]{:S(2)}, u32[]{:S(2)}) collective-permute-start(bf16[2,32,2,2048]{3,2,0,1:T(2,128)(2,1)S(1)} %all_to_all.15), channel_id=1, source_target_pairs={{0,32},{32,64},{64,96},{96,128},{128,160},{160,192},{192,224},{224... | collective-permute-start | bytes 1572872 | tf_op jit(solution)/shard_map/ppermute | solution.py:20
  60.1 8.6 %collective-permute-start.5 = (bf16[2,32,2,2048]{3,2,0,1:T(2,128)(2,1)S(1)}, bf16[2,32,2,2048]{3,2,0,1:T(2,128)(2,1)S(1)}, u32[]{:S(2)}, u32[]{:S(2)}) collective-permute-start(bf16[2,32,2,2048]{3,2,0,1:T(2,128)(2,1)S(1)} %collective-permute-done.4), channel_id=1, source_target_pairs={{0,32},{32,64},{64,96},{96,128},{128,160},{160,192},{192,224},{224... | collective-permute-start | bytes 1572872 | tf_op jit(solution)/shard_map/ppermute | solution.py:20
  62.6 8.6 %collective-permute-start.12 = (bf16[2,32,2,2048]{3,2,0,1:T(2,128)(2,1)S(1)}, bf16[2,32,2,2048]{3,2,0,1:T(2,128)(2,1)S(1)}, u32[]{:S(2)}, u32[]{:S(2)}) collective-permute-start(bf16[2,32,2,2048]{3,2,0,1:T(2,128)(2,1)S(1)} %all_to_all.15), channel_id=1, source_target_pairs={{0,480},{32,0},{64,32},{96,64},{128,96},{160,128},{192,160},{224,1... | collective-permute-start | bytes 1572872 | tf_op jit(solution)/shard_map/ppermute | solution.py:24
  68.7 11.2 %copy-start.1 = (bf16[2,32,2,2048]{3,2,0,1:T(2,128)(2,1)}, bf16[2,32,2,2048]{3,2,0,1:T(2,128)(2,1)S(1)}, u32[]{:S(2)}) copy-start(bf16[2,32,2,2048]{3,2,0,1:T(2,128)(2,1)S(1)} %collective-permute-done.5) | copy-start | bytes 1572868
  68.7 8.6 %collective-permute-start.6 = (bf16[2,32,2,2048]{3,2,0,1:T(2,128)(2,1)S(1)}, bf16[2,32,2,2048]{3,2,0,1:T(2,128)(2,1)S(1)}, u32[]{:S(2)}, u32[]{:S(2)}) collective-permute-start(bf16[2,32,2,2048]{3,2,0,1:T(2,128)(2,1)S(1)} %collective-permute-done.5), channel_id=1, source_target_pairs={{0,32},{32,64},{64,96},{96,128},{128,160},{160,192},{192,224},{224... | collective-permute-start | bytes 1572872 | tf_op jit(solution)/shard_map/ppermute | solution.py:20
  71.2 8.7 %collective-permute-start.13 = (bf16[2,32,2,2048]{3,2,0,1:T(2,128)(2,1)S(1)}, bf16[2,32,2,2048]{3,2,0,1:T(2,128)(2,1)S(1)}, u32[]{:S(2)}, u32[]{:S(2)}) collective-permute-start(bf16[2,32,2,2048]{3,2,0,1:T(2,128)(2,1)S(1)} %collective-permute-done.12), channel_id=1, source_target_pairs={{0,480},{32,0},{64,32},{96,64},{128,96},{160,128},{192,160},{224,1... | collective-permute-start | bytes 1572872 | tf_op jit(solution)/shard_map/ppermute | solution.py:24
  77.3 11.5 %copy-start.5 = (bf16[2,32,2,2048]{3,2,0,1:T(2,128)(2,1)}, bf16[2,32,2,2048]{3,2,0,1:T(2,128)(2,1)S(1)}, u32[]{:S(2)}) copy-start(bf16[2,32,2,2048]{3,2,0,1:T(2,128)(2,1)S(1)} %collective-permute-done.6) | copy-start | bytes 1572868
  77.3 8.6 %collective-permute-start.7 = (bf16[2,32,2,2048]{3,2,0,1:T(2,128)(2,1)S(1)}, bf16[2,32,2,2048]{3,2,0,1:T(2,128)(2,1)S(1)}, u32[]{:S(2)}, u32[]{:S(2)}) collective-permute-start(bf16[2,32,2,2048]{3,2,0,1:T(2,128)(2,1)S(1)} %collective-permute-done.6), channel_id=1, source_target_pairs={{0,32},{32,64},{64,96},{96,128},{128,160},{160,192},{192,224},{224... | collective-permute-start | bytes 1572872 | tf_op jit(solution)/shard_map/ppermute | solution.py:20
  79.9 0.8 copy-start.3
  79.9 8.9 %collective-permute-start.14 = (bf16[2,32,2,2048]{3,2,0,1:T(2,128)(2,1)S(1)}, bf16[2,32,2,2048]{3,2,0,1:T(2,128)(2,1)S(1)}, u32[]{:S(2)}, u32[]{:S(2)}) collective-permute-start(bf16[2,32,2,2048]{3,2,0,1:T(2,128)(2,1)S(1)} %collective-permute-done.13), channel_id=1, source_target_pairs={{0,480},{32,0},{64,32},{96,64},{128,96},{160,128},{192,160},{224,1... | collective-permute-start | bytes 1572872 | tf_op jit(solution)/shard_map/ppermute | solution.py:24
  85.9 21.5 %copy-start.11 = (bf16[2,32,2,2048]{3,2,0,1:T(2,128)(2,1)}, bf16[2,32,2,2048]{3,2,0,1:T(2,128)(2,1)S(1)}, u32[]{:S(2)}) copy-start(bf16[2,32,2,2048]{3,2,0,1:T(2,128)(2,1)S(1)} %collective-permute-done.7) | copy-start | bytes 1572868
  85.9 8.6 %collective-permute-start.8 = (bf16[2,32,2,2048]{3,2,0,1:T(2,128)(2,1)S(1)}, bf16[2,32,2,2048]{3,2,0,1:T(2,128)(2,1)S(1)}, u32[]{:S(2)}, u32[]{:S(2)}) collective-permute-start(bf16[2,32,2,2048]{3,2,0,1:T(2,128)(2,1)S(1)} %collective-permute-done.7), channel_id=1, source_target_pairs={{0,32},{32,64},{64,96},{96,128},{128,160},{160,192},{192,224},{224... | collective-permute-start | bytes 1572872 | tf_op jit(solution)/shard_map/ppermute | solution.py:20
  88.8 1.4 copy-start.7
  88.8 8.9 %collective-permute-start.15 = (bf16[2,32,2,2048]{3,2,0,1:T(2,128)(2,1)S(1)}, bf16[2,32,2,2048]{3,2,0,1:T(2,128)(2,1)S(1)}, u32[]{:S(2)}, u32[]{:S(2)}) collective-permute-start(bf16[2,32,2,2048]{3,2,0,1:T(2,128)(2,1)S(1)} %collective-permute-done.14), channel_id=1, source_target_pairs={{0,480},{32,0},{64,32},{96,64},{128,96},{160,128},{192,160},{224,1... | collective-permute-start | bytes 1572872 | tf_op jit(solution)/shard_map/ppermute | solution.py:24
  94.5 15.9 %copy-start.13 = (bf16[2,32,2,2048]{3,2,0,1:T(2,128)(2,1)}, bf16[2,32,2,2048]{3,2,0,1:T(2,128)(2,1)S(1)}, u32[]{:S(2)}) copy-start(bf16[2,32,2,2048]{3,2,0,1:T(2,128)(2,1)S(1)} %collective-permute-done.8) | copy-start | bytes 1572868
  94.5 8.6 %collective-permute-start.9 = (bf16[2,32,2,2048]{3,2,0,1:T(2,128)(2,1)S(1)}, bf16[2,32,2,2048]{3,2,0,1:T(2,128)(2,1)S(1)}, u32[]{:S(2)}, u32[]{:S(2)}) collective-permute-start(bf16[2,32,2,2048]{3,2,0,1:T(2,128)(2,1)S(1)} %collective-permute-done.8), channel_id=1, source_target_pairs={{0,32},{32,64},{64,96},{96,128},{128,160},{160,192},{192,224},{224... | collective-permute-start | bytes 1572872 | tf_op jit(solution)/shard_map/ppermute | solution.py:20
  97.7 0.8 copy-start.9
  98.5 8.9 %collective-permute-start.16 = (bf16[2,32,2,2048]{3,2,0,1:T(2,128)(2,1)S(1)}, bf16[2,32,2,2048]{3,2,0,1:T(2,128)(2,1)}, u32[]{:S(2)}, u32[]{:S(2)}) collective-permute-start(bf16[2,32,2,2048]{3,2,0,1:T(2,128)(2,1)S(1)} %collective-permute-done.15), channel_id=1, source_target_pairs={{0,480},{32,0},{64,32},{96,64},{128,96},{160,128},{192,160},{224,1... | collective-permute-start | bytes 1572872 | tf_op jit(solution)/shard_map/ppermute | solution.py:24
  103.1 8.6 %copy-start.15 = (bf16[2,32,2,2048]{3,2,0,1:T(2,128)(2,1)}, bf16[2,32,2,2048]{3,2,0,1:T(2,128)(2,1)S(1)}, u32[]{:S(2)}) copy-start(bf16[2,32,2,2048]{3,2,0,1:T(2,128)(2,1)S(1)} %collective-permute-done.9) | copy-start | bytes 1572868
  103.1 8.6 %collective-permute-start.10 = (bf16[2,32,2,2048]{3,2,0,1:T(2,128)(2,1)S(1)}, bf16[2,32,2,2048]{3,2,0,1:T(2,128)(2,1)}, u32[]{:S(2)}, u32[]{:S(2)}) collective-permute-start(bf16[2,32,2,2048]{3,2,0,1:T(2,128)(2,1)S(1)} %collective-permute-done.9), channel_id=1, source_target_pairs={{0,32},{32,64},{64,96},{96,128},{128,160},{160,192},{192,224},{224... | collective-permute-start | bytes 1572872 | tf_op jit(solution)/shard_map/ppermute | solution.py:20
  107.4 9.2 %collective-permute-start.17 = (bf16[2,32,2,2048]{3,2,0,1:T(2,128)(2,1)}, bf16[2,32,2,2048]{3,2,0,1:T(2,128)(2,1)}, u32[]{:S(2)}, u32[]{:S(2)}) collective-permute-start(bf16[2,32,2,2048]{3,2,0,1:T(2,128)(2,1)} %collective-permute-done.16), channel_id=1, source_target_pairs={{0,480},{32,0},{64,32},{96,64},{128,96},{160,128},{192,160},{224,1... | collective-permute-start | bytes 1572872 | tf_op jit(solution)/shard_map/ppermute | solution.py:24
  111.7 9.7 %collective-permute-start.11 = (bf16[2,32,2,2048]{3,2,0,1:T(2,128)(2,1)}, bf16[2,32,2,2048]{3,2,0,1:T(2,128)(2,1)}, u32[]{:S(2)}, u32[]{:S(2)}) collective-permute-start(bf16[2,32,2,2048]{3,2,0,1:T(2,128)(2,1)} %collective-permute-done.10), channel_id=1, source_target_pairs={{0,32},{32,64},{64,96},{96,128},{128,160},{160,192},{192,224},{224... | collective-permute-start | bytes 1572872 | tf_op jit(solution)/shard_map/ppermute | solution.py:20
  114.3 44.1 %copy-start.16 = (bf16[2,32,2,2048]{3,2,0,1:T(2,128)(2,1)S(1)}, bf16[2,32,2,2048]{3,2,0,1:T(2,128)(2,1)}, u32[]{:S(2)}) copy-start(bf16[2,32,2,2048]{3,2,0,1:T(2,128)(2,1)} %copy-done.15) | copy-start | bytes 1572868
  114.3 45.4 %copy-start.14 = (bf16[2,32,2,2048]{3,2,0,1:T(2,128)(2,1)S(1)}, bf16[2,32,2,2048]{3,2,0,1:T(2,128)(2,1)}, u32[]{:S(2)}) copy-start(bf16[2,32,2,2048]{3,2,0,1:T(2,128)(2,1)} %copy-done.13) | copy-start | bytes 1572868
  114.3 46.6 %copy-start.12 = (bf16[2,32,2,2048]{3,2,0,1:T(2,128)(2,1)S(1)}, bf16[2,32,2,2048]{3,2,0,1:T(2,128)(2,1)}, u32[]{:S(2)}) copy-start(bf16[2,32,2,2048]{3,2,0,1:T(2,128)(2,1)} %copy-done.11) | copy-start | bytes 1572868
  114.3 47.9 %copy-start.6 = (bf16[2,32,2,2048]{3,2,0,1:T(2,128)(2,1)S(1)}, bf16[2,32,2,2048]{3,2,0,1:T(2,128)(2,1)}, u32[]{:S(2)}) copy-start(bf16[2,32,2,2048]{3,2,0,1:T(2,128)(2,1)} %copy-done.5) | copy-start | bytes 1572868
  114.3 49.1 %copy-start.2 = (bf16[2,32,2,2048]{3,2,0,1:T(2,128)(2,1)S(1)}, bf16[2,32,2,2048]{3,2,0,1:T(2,128)(2,1)}, u32[]{:S(2)}) copy-start(bf16[2,32,2,2048]{3,2,0,1:T(2,128)(2,1)} %copy-done.1) | copy-start | bytes 1572868
  114.3 54.2 %copy-start.4 = (bf16[2,32,2,2048]{3,2,0,1:T(2,128)(2,1)S(1)}, bf16[2,32,2,2048]{3,2,0,1:T(2,128)(2,1)}, u32[]{:S(2)}) copy-start(bf16[2,32,2,2048]{3,2,0,1:T(2,128)(2,1)} %copy-done.3) | copy-start | bytes 1572868
  114.3 55.5 %copy-start.8 = (bf16[2,32,2,2048]{3,2,0,1:T(2,128)(2,1)S(1)}, bf16[2,32,2,2048]{3,2,0,1:T(2,128)(2,1)}, u32[]{:S(2)}) copy-start(bf16[2,32,2,2048]{3,2,0,1:T(2,128)(2,1)} %copy-done.7) | copy-start | bytes 1572868
  114.4 56.7 %copy-start.10 = (bf16[2,32,2,2048]{3,2,0,1:T(2,128)(2,1)S(1)}, bf16[2,32,2,2048]{3,2,0,1:T(2,128)(2,1)}, u32[]{:S(2)}) copy-start(bf16[2,32,2,2048]{3,2,0,1:T(2,128)(2,1)} %copy-done.9) | copy-start | bytes 1572868
  116.6 35.9 %collective-permute-start.18 = (bf16[2,32,2,2048]{3,2,0,1:T(2,128)(2,1)}, bf16[2,32,2,2048]{3,2,0,1:T(2,128)(2,1)S(1)}, u32[]{:S(2)}, u32[]{:S(2)}) collective-permute-start(bf16[2,32,2,2048]{3,2,0,1:T(2,128)(2,1)} %collective-permute-done.17), channel_id=1, source_target_pairs={{0,480},{32,0},{64,32},{96,64},{128,96},{160,128},{192,160},{224,1... | collective-permute-start | bytes 1572872 | tf_op jit(solution)/shard_map/ppermute | solution.py:24
  196.4 138.7 %copy-start.17 = (s32[48,2]{0,1:T(2,128)S(1)}, s32[48,2]{0,1:T(2,128)}, u32[]{:S(2)}) copy-start(s32[48,2]{0,1:T(2,128)} %param.12) | copy-start | bytes 1156
  330.8 21.8 %all-to-all-start.2 = ((bf16[2,32,2,2048]{3,2,0,1:T(2,128)(2,1)}), bf16[2,32,2,2048]{3,2,0,1:T(2,128)(2,1)S(1)}, u32[]{:S(2)}, u32[]{:S(2)}) async-start(bf16[2,32,2,2048]{3,2,0,1:T(2,128)(2,1)} %copy.70), calls=%async_computation.2 | async-start | bytes 1048576 | tf_op jit(solution)/shard_map/all_to_all | solution.py:110
